TPU v7x, 128 devices: a whole 4x4x4 slice. The times are simulated.
128 devices in a mesh: grp: 16 (over z, x), tp: 8 (over y, core).
Axes of the slice: x: 4, y: 4, z: 4, core: 2. Of those that a mesh axis runs over, the one named last changes fastest.
Arguments:
- hidden: bfloat16 [8192, 12288], P('grp', 'tp'), may hold values from -6 to 6
- queries: bfloat16 [8192, 12288], P('grp', 'tp'), may hold values from -25 to 25
- keyval_weight: bfloat16 [12288, 2, 1024], P(None, None, 'tp'), may hold values from -0.0546875 to 0.0546875
- keyval_pool: bfloat16 [1280, 2, 8, 128, 128], P('grp', None, 'tp'), may hold values from -6 to 6
- prefix_len: int32 [32], replicated, may hold values from 128 to 4096, as said below
- slot_request: int32 [32], replicated, may hold values from 0 to 31, as said below
- hit_holder: int32 [32, 32], replicated, may hold values from 0 to 15, as said below
- hit_slot: int32 [32, 32], replicated, may hold values from 0 to 79, as said below
- new_owner: int32 [32, 2], replicated, may hold values from 0 to 15, as said below
- new_slot: int32 [32, 2], replicated, may hold values from 0 to 79, as said below
Outputs:
- attention: bfloat16 [8192, 12288], P('grp', 'tp')
- new_pool: bfloat16 [1280, 2, 8, 128, 128], P('grp', None, 'tp')
Inputs may be any that keep to these rules, and one draw needn't show every extreme that they name: `prefix_len`: every request of some group (slots g * 2 to g * 2 + 1) has exactly 4096. `slot_request`: a permutation; group g serves the requests in slots g * 2 to g * 2 + 1, and its rows of hidden and queries stand in that order. `hit_holder`: block b of request r is live iff b * 128 < prefix_len[r]; other entries are to be ignored. Among all 64 entries of one group's requests, live or not, no holder is named more than 4 times, and in the group whose prefixes are full some holder is named exactly 4 times. `hit_slot`: all entries name different pool rows, none of them a row that new_owner and new_slot name. `new_owner`: the 4 new blocks of one group's requests have different owners. `new_slot`: all new blocks name different pool rows.
All inputs are finite; a program needn't handle non-finite values.
Results may differ from a plain program's by a relative error of at most 0.025.
Values may be sent and summed in bfloat16 or wider, within the bound.
A program may use at most 128 MiB of HBM per device.

v0:
```python
import math

import jax
import jax.numpy as jnp
from jax import lax
from jax.sharding import PartitionSpec as P

ROPE_BASE = 1000000.0
MASKED_SCORE = -1e30


def rotate(key_block, positions):
    half_dim = key_block.shape[-1] // 2
    frequency = ROPE_BASE ** (
        -(jnp.arange(half_dim, dtype=jnp.float32) * 2.0 / key_block.shape[-1])
    )
    angles = positions.astype(jnp.float32)[:, None] * frequency[None, :]
    cosine = jnp.cos(angles)
    sine_part = jnp.sin(angles)
    front_half = key_block[..., :half_dim]
    back_half = key_block[..., half_dim:]
    return jnp.concatenate(
        [front_half * cosine - back_half * sine_part, back_half * cosine + front_half * sine_part],
        axis=-1,
    )


def block_ranks(requests, prefix_len, hit_holder, groups, block_len):
    lengths = prefix_len[requests]
    block_count = hit_holder.shape[1]
    is_live = (
        jnp.arange(block_count, dtype=jnp.int32)[None, :] * block_len < lengths[:, None]
    ).reshape(-1)
    holders = hit_holder[requests].reshape(-1)
    marks = (
        (holders[:, None] == jnp.arange(groups, dtype=jnp.int32)[None, :]) & is_live[:, None]
    ).astype(jnp.int32)
    before = jnp.cumsum(marks, axis=0) - marks
    rank_of = jnp.sum(before * marks, axis=1)
    return (is_live, holders, rank_of)


def per_device(
    hidden,
    queries,
    keyval_weight,
    keyval_pool,
    prefix_len,
    slot_request,
    hit_holder,
    hit_slot,
    new_owner,
    new_slot,
):
    groups = lax.axis_size("grp")
    my_group = lax.axis_index("grp")
    token_rows = hidden.shape[0]
    per_group = slot_request.shape[0] // groups
    stretch_len = token_rows // per_group
    pool_slots = keyval_pool.shape[0]
    kv_local = keyval_pool.shape[2]
    block_len = keyval_pool.shape[3]
    head_dim = keyval_pool.shape[4]
    capacity = pool_slots // groups - 1
    block_count = hit_holder.shape[1]
    fresh_count = new_owner.shape[1] * per_group
    grouping = queries.shape[1] // (kv_local * head_dim)
    score_scale = 1.0 / math.sqrt(head_dim)
    my_requests = lax.dynamic_slice_in_dim(slot_request, my_group * per_group, per_group)
    my_lengths = prefix_len[my_requests]
    shard_piece = lax.all_gather(hidden, "tp", axis=1, tiled=True)
    row_block = keyval_weight
    row_block = row_block.reshape(shard_piece.shape[1], 2, kv_local, head_dim)
    projected = jnp.einsum(
        "td,dcjh->jtch", shard_piece, row_block, preferred_element_type=jnp.float32
    )
    token_index = jnp.arange(token_rows, dtype=jnp.int32)
    positions = my_lengths[token_index // stretch_len] + token_index % stretch_len
    stretch_keys = rotate(projected[:, :, 0], positions).astype(jnp.bfloat16)
    stretch_values = projected[:, :, 1].astype(jnp.bfloat16)
    block_keys = stretch_keys.reshape(kv_local, fresh_count, block_len, head_dim)
    block_values = stretch_values.reshape(kv_local, fresh_count, block_len, head_dim)
    pushed_owner = new_owner[my_requests].reshape(-1)
    selector = (jnp.arange(groups, dtype=jnp.int32)[:, None] == pushed_owner[None, :]).astype(
        jnp.bfloat16
    )
    push_keys = jnp.einsum(
        "oe,jebh->ojbh", selector, block_keys, preferred_element_type=jnp.float32
    )
    push_values = jnp.einsum(
        "oe,jebh->ojbh", selector, block_values, preferred_element_type=jnp.float32
    )
    push_send = jnp.stack([push_keys, push_values], axis=1).astype(jnp.bfloat16)[:, None]
    every_group = slot_request.reshape(groups, per_group)

    def outgoing(requests):
        is_live, holders, rank_of = block_ranks(requests, prefix_len, hit_holder, groups, block_len)
        slot_ids = hit_slot[requests].reshape(-1)
        chosen = (is_live & (holders == my_group))[:, None] & (
            rank_of[:, None] == jnp.arange(capacity, dtype=jnp.int32)[None, :]
        )
        return (jnp.sum(jnp.where(chosen, slot_ids[:, None], 0), axis=0), jnp.any(chosen, axis=0))

    send_rows, filled = jax.vmap(outgoing)(every_group)
    fetched = keyval_pool[send_rows.reshape(-1)].reshape((groups, capacity) + keyval_pool.shape[1:])
    pull_send = jnp.where(
        filled[:, :, None, None, None, None], fetched, jnp.zeros((), jnp.bfloat16)
    )
    received = lax.all_to_all(pull_send, "grp", split_axis=0, concat_axis=0, tiled=True)
    pushed = lax.all_to_all(push_send, "grp", split_axis=0, concat_axis=0, tiled=True)
    all_owner = new_owner[slot_request].reshape(groups, -1)
    all_slot = new_slot[slot_request].reshape(groups, -1)
    owned = all_owner == my_group
    target = jnp.where(
        jnp.any(owned, axis=1), jnp.sum(jnp.where(owned, all_slot, 0), axis=1), pool_slots
    )
    new_pool = keyval_pool.at[target].set(pushed[:, 0], mode="drop")
    is_live, holders, rank_of = block_ranks(my_requests, prefix_len, hit_holder, groups, block_len)
    arrived = received.reshape((groups * capacity,) + keyval_pool.shape[1:])[
        holders * capacity + rank_of
    ]
    prefix_blocks = arrived.reshape((per_group, block_count) + keyval_pool.shape[1:])
    query_rows = queries.reshape(per_group, stretch_len, kv_local, grouping, head_dim)
    keys_by_request = stretch_keys.reshape(kv_local, per_group, stretch_len, head_dim)
    values_by_request = stretch_values.reshape(kv_local, per_group, stretch_len, head_dim)
    scores = (
        jnp.einsum(
            "rtjgd,jrkd->rjtgk", query_rows, keys_by_request, preferred_element_type=jnp.float32
        )
        * score_scale
    )
    causal = (jnp.arange(stretch_len)[None, :] <= jnp.arange(stretch_len)[:, None])[
        None, None, :, None, :
    ]
    scores = jnp.where(causal, scores, MASKED_SCORE)
    row_max = jnp.max(scores, axis=-1)
    weights = jnp.where(causal, jnp.exp(scores - row_max[..., None]), 0.0)
    weight_sum = jnp.sum(weights, axis=-1)
    weighted = jnp.einsum(
        "rjtgk,jrkd->rjtgd",
        weights.astype(jnp.bfloat16),
        values_by_request,
        preferred_element_type=jnp.float32,
    )
    key_step = 4
    span_keys = key_step * block_len

    def visit(turn_index, state_now):
        running_max, running_sum, running_out = state_now
        key_part = lax.dynamic_slice_in_dim(prefix_blocks, turn_index * key_step, key_step, 1)
        block_scores = jnp.einsum(
            "rtjgd,rbjkd->rjtgbk", query_rows, key_part[:, :, 0], preferred_element_type=jnp.float32
        )
        block_scores = (
            block_scores.reshape(per_group, kv_local, stretch_len, grouping, span_keys)
            * score_scale
        )
        key_index = turn_index * span_keys + jnp.arange(span_keys, dtype=jnp.int32)
        visible = (key_index[None, :] < my_lengths[:, None])[:, None, None, None, :]
        block_scores = jnp.where(visible, block_scores, MASKED_SCORE)
        new_max = jnp.maximum(running_max, jnp.max(block_scores, axis=-1))
        rescale = jnp.exp(running_max - new_max)
        block_weights = jnp.where(visible, jnp.exp(block_scores - new_max[..., None]), 0.0)
        running_sum = running_sum * rescale + jnp.sum(block_weights, axis=-1)
        block_weights = block_weights.astype(jnp.bfloat16).reshape(
            per_group, kv_local, stretch_len, grouping, key_step, block_len
        )
        running_out = running_out * rescale[..., None] + jnp.einsum(
            "rjtgbk,rbjkd->rjtgd",
            block_weights,
            key_part[:, :, 1],
            preferred_element_type=jnp.float32,
        )
        return (new_max, running_sum, running_out)

    last_turn = block_count // key_step
    row_max, weight_sum, weighted = lax.fori_loop(
        0, last_turn, visit, (row_max, weight_sum, weighted)
    )
    combined = weighted / weight_sum[..., None]
    attention = (
        jnp.transpose(combined, (0, 2, 1, 3, 4)).reshape(token_rows, -1).astype(jnp.bfloat16)
    )
    return (attention, new_pool)


def solution(mesh):
    in_specs = (
        P("grp", "tp"),
        P("grp", "tp"),
        P(None, None, "tp"),
        P("grp", None, "tp", None, None),
        P(),
        P(),
        P(),
        P(),
        P(),
        P(),
    )
    out_specs = (P("grp", "tp"), P("grp", None, "tp", None, None))
    return jax.shard_map(
        per_device, mesh=mesh, in_specs=in_specs, out_specs=out_specs, check_vma=False
    )
```

profile of v0, /device:TPU:1, one launch (start us, length us, event | category | flops | bytes accessed | tf_op | source)
XLA Modules:
  0.0 263.0 jit_solution(10739946615628425059)
XLA Ops:
  7.2 7.0 %copy.184 = bf16[80,2,1,128,128]{4,3,2,1,0:T(8,128)(2,1)} copy(bf16[80,2,1,128,128]{4,3,2,1,0:T(8,128)(2,1)} %param.15) | data formatting | bytes 10485760
  19.4 5.5 %gather_fusion.4 = bf16[64,2,128,128]{3,2,1,0:T(8,128)(2,1)} fusion(bf16[80,2,128,128]{3,2,1,0:T(8,128)(2,1)} %bitcast.173, s32[1024]{0:T(1024)S(1)} %pad_clamp_fusion.2), kind=kCustom, calls=%fused_computation.4 | custom fusion | bytes 8388864 | tf_op jit(solution)/shard_map/gather | solution.py:105
  24.9 4.8 %broadcast_select_fusion = bf16[16,4,2,1,128,128]{5,4,2,1,3,0:T(8,128)(2,1)} fusion(bf16[16,4,2,1,128,128]{5,4,2,1,3,0:T(8,128)(2,1)} %bitcast.176, pred[16,4]{1,0:T(8,128)(4,1)S(1)} %copy.122), kind=kLoop, calls=%fused_computation.45 | loop fusion | flops 2097152 | bytes 8388672 | tf_op jit(solution)/shard_map/jit(_where)/select_n | solution.py:106
  29.7 9.2 %all-to-all-start = ((bf16[16,4,2,1,128,128]{5,4,2,1,3,0:T(8,128)(2,1)}), bf16[16,4,2,1,128,128]{5,4,2,1,3,0:T(8,128)(2,1)}, u32[]{:S(2)}, u32[]{:S(2)}) async-start(bf16[16,4,2,1,128,128]{5,4,2,1,3,0:T(8,128)(2,1)} %broadcast_select_fusion), calls=%async_computation | async-start | bytes 8388608 | tf_op jit(solution)/shard_map/all_to_all | solution.py:109
  51.7 49.8 %all-to-all-done = bf16[16,4,2,1,128,128]{5,4,2,1,3,0:T(8,128)(2,1)} async-done(((bf16[16,4,2,1,128,128]{5,4,2,1,3,0:T(8,128)(2,1)}), bf16[16,4,2,1,128,128]{5,4,2,1,3,0:T(8,128)(2,1)}, u32[]{:S(2)}, u32[]{:S(2)}) %all-to-all-start) | async-done | bytes 4194336 | tf_op jit(solution)/shard_map/all_to_all | solution.py:109
  101.4 5.2 %gather_fusion.6 = bf16[64,2,128,128]{3,2,1,0:T(8,128)(2,1)} fusion(bf16[64,2,128,128]{3,2,1,0:T(8,128)(2,1)} %bitcast.40, s32[1024]{0:T(1024)S(1)} %pad_clamp_fusion.1), kind=kCustom, calls=%fused_computation.6 | custom fusion | bytes 8388864 | tf_op jit(solution)/shard_map/gather | solution.py:119
  106.7 8.3 %fusion.38 = f32[1,512,2,128]{1,3,2,0:T(8,128)S(1)} fusion(bf16[512,12288]{1,0:T(8,128)(2,1)} %all-gather.2.cloned.1.call-done, bf16[12288,2,128]{2,1,0:T(2,128)(2,1)} %param.14), kind=kOutput, calls=%fused_computation.61 | convolution fusion | flops 3221225472 | bytes 19398656 | tf_op jit(solution)/shard_map/td,dcjh->jtch/dot_general | solution.py:74
  118.9 4.6 %all-to-all-start.1 = ((bf16[16,1,2,1,128,128]{5,4,3,2,1,0:T(8,128)(2,1)}), bf16[16,1,2,1,128,128]{5,4,3,2,1,0:T(8,128)(2,1)S(1)}, u32[]{:S(2)}, u32[]{:S(2)}) async-start(bf16[16,1,2,1,128,128]{5,4,3,2,1,0:T(8,128)(2,1)} %copy.135), calls=%async_computation.1 | async-start | bytes 2097152 | tf_op jit(solution)/shard_map/all_to_all | solution.py:110
  128.3 3.7 %fusion.31 = f32[2,1,256,12,128]{4,2,3,0,1:T(8,128)} fusion(bf16[2,256,128,1]{2,1,3,0:T(8,128)(2,1)S(1)} %bitcast.188, f32[2,256,256,12]{2,1,3,0:T(8,128)S(1)} %get-tuple-element.192, f32[2,256,12]{1,2,0:T(8,128)S(1)} %get-tuple-element.191, pred[256,256]{0,1:T(8,128)(4,1)S(1)} %iota_compare_fusion.1), kind=kOutput, calls=%fused_computation.53 | convolution fusion | flops 410517504 | bytes 9658368 | tf_op jit(solution)/shard_map/rjtgk,jrkd->rjtgd/dot_general | solution.py:139
  132.0 115.9 %while.17 = (s32[]{:T(128)}, f32[2,1,256,12]{2,3,0,1:T(8,128)S(1)}, f32[2,1,256,12]{2,3,0,1:T(8,128)S(1)}, f32[2,1,256,12,128]{4,2,3,0,1:T(8,128)}, s32[2]{0:T(1...) while((s32[]{:T(128)}, f32[2,1,256,12]{2,3,0,1:T(8,128)S(1)}, ...), condition=%wide.region_11.12_spmd, body=%wide.region_8.11_spmd.sunk | while | flops 1653101056 | bytes 71722264 | solution.py:177
  135.2 3.4 %fusion.94 = f32[2,256,12]{1,2,0:T(8,128)S(1)} fusion(f32[2,4,128,256,12]{3,2,4,1,0:T(8,128)S(1)} %get-tuple-element.242, f32[2,256,12]{1,2,0:T(8,128)S(1)} %bitcast.177, pred[2,4,128]{2,1,0:T(4,128)(4,1)S(1)} %broadcast_compare_fusion.6), kind=kLoop, calls=%fused_computation.17.clone.1 | loop fusion | flops 15722496 | bytes 12633088 | tf_op jit(solution)/shard_map/while/body/eval_jaxpr/reduce_sum | solution.py:164
  138.6 6.2 %bitcast_add_fusion.6 = f32[2,1,256,12,128]{4,2,3,0,1:T(8,128)S(1)} fusion(f32[2,1,256,12,128]{4,2,3,0,1:T(8,128)S(1)} %copy-done.4, f32[2,4,128,256,12]{3,2,4,1,0:T(8,128)S(1)} %get-tuple-element.242, f32[2,256,12]{1,2,0:T(8,128)S(1)} %bitcast.178, pred[2,4,128]{2,1,0:T(4,128)(4,1)S(1)} %broadcast_compare_fusion.6, ...), kind=kOutput, calls=%fused_computation.21.clone.1 | convolution fusion | flops 822607872 | bytes 19204104 | tf_op jit(solution)/shard_map/while/body/eval_jaxpr/rjtgbk,rbjkd->rjtgd/dot_general | solution.py:168
  149.7 3.4 %fusion.94 = f32[2,256,12]{1,2,0:T(8,128)S(1)} fusion(f32[2,4,128,256,12]{3,2,4,1,0:T(8,128)S(1)} %get-tuple-element.242, f32[2,256,12]{1,2,0:T(8,128)S(1)} %bitcast.177, pred[2,4,128]{2,1,0:T(4,128)(4,1)S(1)} %broadcast_compare_fusion.6), kind=kLoop, calls=%fused_computation.17.clone.1 | loop fusion | flops 15722496 | bytes 12633088 | tf_op jit(solution)/shard_map/while/body/eval_jaxpr/reduce_sum | solution.py:164
  153.1 6.2 %bitcast_add_fusion.6 = f32[2,1,256,12,128]{4,2,3,0,1:T(8,128)S(1)} fusion(f32[2,1,256,12,128]{4,2,3,0,1:T(8,128)S(1)} %copy-done.4, f32[2,4,128,256,12]{3,2,4,1,0:T(8,128)S(1)} %get-tuple-element.242, f32[2,256,12]{1,2,0:T(8,128)S(1)} %bitcast.178, pred[2,4,128]{2,1,0:T(4,128)(4,1)S(1)} %broadcast_compare_fusion.6, ...), kind=kOutput, calls=%fused_computation.21.clone.1 | convolution fusion | flops 822607872 | bytes 19204104 | tf_op jit(solution)/shard_map/while/body/eval_jaxpr/rjtgbk,rbjkd->rjtgd/dot_general | solution.py:168
  161.0 3.1 %bitcast_reduce_fusion.2 = (f32[2,256,12]{1,2,0:T(8,128)S(1)}, f32[2,4,128,256,12]{3,2,4,1,0:T(8,128)S(1)}) fusion(pred[2,4,128]{2,1,0:T(4,128)(4,1)S(1)} %broadcast_compare_fusion.6, bf16[2,256,1,12,128]{4,1,3,0,2:T(8,128)(2,1)S(1)} %get-tuple-element.276, bf16[2,32,2,1,128,128]{5,4,2,1,0,3:T(8,128)(2,1)} %get-tuple-element.275, s32[]{:T(128)S(6)} %select_n.274), kind=kOutput, calls=%fused_computation.12.clone.1 | convolution fusion | flops 814737408 | bytes 14443524 | tf_op jit(solution)/shard_map/while/body/eval_jaxpr/rtjgd,rbjkd->rjtgbk/dot_general | solution.py:151
  164.2 3.4 %fusion.94 = f32[2,256,12]{1,2,0:T(8,128)S(1)} fusion(f32[2,4,128,256,12]{3,2,4,1,0:T(8,128)S(1)} %get-tuple-element.242, f32[2,256,12]{1,2,0:T(8,128)S(1)} %bitcast.177, pred[2,4,128]{2,1,0:T(4,128)(4,1)S(1)} %broadcast_compare_fusion.6), kind=kLoop, calls=%fused_computation.17.clone.1 | loop fusion | flops 15722496 | bytes 12633088 | tf_op jit(solution)/shard_map/while/body/eval_jaxpr/reduce_sum | solution.py:164
  167.6 6.2 %bitcast_add_fusion.6 = f32[2,1,256,12,128]{4,2,3,0,1:T(8,128)S(1)} fusion(f32[2,1,256,12,128]{4,2,3,0,1:T(8,128)S(1)} %copy-done.4, f32[2,4,128,256,12]{3,2,4,1,0:T(8,128)S(1)} %get-tuple-element.242, f32[2,256,12]{1,2,0:T(8,128)S(1)} %bitcast.178, pred[2,4,128]{2,1,0:T(4,128)(4,1)S(1)} %broadcast_compare_fusion.6, ...), kind=kOutput, calls=%fused_computation.21.clone.1 | convolution fusion | flops 822607872 | bytes 19204104 | tf_op jit(solution)/shard_map/while/body/eval_jaxpr/rjtgbk,rbjkd->rjtgd/dot_general | solution.py:168
  175.5 3.1 %bitcast_reduce_fusion.2 = (f32[2,256,12]{1,2,0:T(8,128)S(1)}, f32[2,4,128,256,12]{3,2,4,1,0:T(8,128)S(1)}) fusion(pred[2,4,128]{2,1,0:T(4,128)(4,1)S(1)} %broadcast_compare_fusion.6, bf16[2,256,1,12,128]{4,1,3,0,2:T(8,128)(2,1)S(1)} %get-tuple-element.276, bf16[2,32,2,1,128,128]{5,4,2,1,0,3:T(8,128)(2,1)} %get-tuple-element.275, s32[]{:T(128)S(6)} %select_n.274), kind=kOutput, calls=%fused_computation.12.clone.1 | convolution fusion | flops 814737408 | bytes 14443524 | tf_op jit(solution)/shard_map/while/body/eval_jaxpr/rtjgd,rbjkd->rjtgbk/dot_general | solution.py:151
  178.7 3.4 %fusion.94 = f32[2,256,12]{1,2,0:T(8,128)S(1)} fusion(f32[2,4,128,256,12]{3,2,4,1,0:T(8,128)S(1)} %get-tuple-element.242, f32[2,256,12]{1,2,0:T(8,128)S(1)} %bitcast.177, pred[2,4,128]{2,1,0:T(4,128)(4,1)S(1)} %broadcast_compare_fusion.6), kind=kLoop, calls=%fused_computation.17.clone.1 | loop fusion | flops 15722496 | bytes 12633088 | tf_op jit(solution)/shard_map/while/body/eval_jaxpr/reduce_sum | solution.py:164
  182.1 6.2 %bitcast_add_fusion.6 = f32[2,1,256,12,128]{4,2,3,0,1:T(8,128)S(1)} fusion(f32[2,1,256,12,128]{4,2,3,0,1:T(8,128)S(1)} %copy-done.4, f32[2,4,128,256,12]{3,2,4,1,0:T(8,128)S(1)} %get-tuple-element.242, f32[2,256,12]{1,2,0:T(8,128)S(1)} %bitcast.178, pred[2,4,128]{2,1,0:T(4,128)(4,1)S(1)} %broadcast_compare_fusion.6, ...), kind=kOutput, calls=%fused_computation.21.clone.1 | convolution fusion | flops 822607872 | bytes 19204104 | tf_op jit(solution)/shard_map/while/body/eval_jaxpr/rjtgbk,rbjkd->rjtgd/dot_general | solution.py:168
  190.0 3.1 %bitcast_reduce_fusion.2 = (f32[2,256,12]{1,2,0:T(8,128)S(1)}, f32[2,4,128,256,12]{3,2,4,1,0:T(8,128)S(1)}) fusion(pred[2,4,128]{2,1,0:T(4,128)(4,1)S(1)} %broadcast_compare_fusion.6, bf16[2,256,1,12,128]{4,1,3,0,2:T(8,128)(2,1)S(1)} %get-tuple-element.276, bf16[2,32,2,1,128,128]{5,4,2,1,0,3:T(8,128)(2,1)} %get-tuple-element.275, s32[]{:T(128)S(6)} %select_n.274), kind=kOutput, calls=%fused_computation.12.clone.1 | convolution fusion | flops 814737408 | bytes 14443524 | tf_op jit(solution)/shard_map/while/body/eval_jaxpr/rtjgd,rbjkd->rjtgbk/dot_general | solution.py:151
  193.1 3.4 %fusion.94 = f32[2,256,12]{1,2,0:T(8,128)S(1)} fusion(f32[2,4,128,256,12]{3,2,4,1,0:T(8,128)S(1)} %get-tuple-element.242, f32[2,256,12]{1,2,0:T(8,128)S(1)} %bitcast.177, pred[2,4,128]{2,1,0:T(4,128)(4,1)S(1)} %broadcast_compare_fusion.6), kind=kLoop, calls=%fused_computation.17.clone.1 | loop fusion | flops 15722496 | bytes 12633088 | tf_op jit(solution)/shard_map/while/body/eval_jaxpr/reduce_sum | solution.py:164
  196.6 6.2 %bitcast_add_fusion.6 = f32[2,1,256,12,128]{4,2,3,0,1:T(8,128)S(1)} fusion(f32[2,1,256,12,128]{4,2,3,0,1:T(8,128)S(1)} %copy-done.4, f32[2,4,128,256,12]{3,2,4,1,0:T(8,128)S(1)} %get-tuple-element.242, f32[2,256,12]{1,2,0:T(8,128)S(1)} %bitcast.178, pred[2,4,128]{2,1,0:T(4,128)(4,1)S(1)} %broadcast_compare_fusion.6, ...), kind=kOutput, calls=%fused_computation.21.clone.1 | convolution fusion | flops 822607872 | bytes 19204104 | tf_op jit(solution)/shard_map/while/body/eval_jaxpr/rjtgbk,rbjkd->rjtgd/dot_general | solution.py:168
  204.5 3.1 %bitcast_reduce_fusion.2 = (f32[2,256,12]{1,2,0:T(8,128)S(1)}, f32[2,4,128,256,12]{3,2,4,1,0:T(8,128)S(1)}) fusion(pred[2,4,128]{2,1,0:T(4,128)(4,1)S(1)} %broadcast_compare_fusion.6, bf16[2,256,1,12,128]{4,1,3,0,2:T(8,128)(2,1)S(1)} %get-tuple-element.276, bf16[2,32,2,1,128,128]{5,4,2,1,0,3:T(8,128)(2,1)} %get-tuple-element.275, s32[]{:T(128)S(6)} %select_n.274), kind=kOutput, calls=%fused_computation.12.clone.1 | convolution fusion | flops 814737408 | bytes 14443524 | tf_op jit(solution)/shard_map/while/body/eval_jaxpr/rtjgd,rbjkd->rjtgbk/dot_general | solution.py:151
  207.6 3.4 %fusion.94 = f32[2,256,12]{1,2,0:T(8,128)S(1)} fusion(f32[2,4,128,256,12]{3,2,4,1,0:T(8,128)S(1)} %get-tuple-element.242, f32[2,256,12]{1,2,0:T(8,128)S(1)} %bitcast.177, pred[2,4,128]{2,1,0:T(4,128)(4,1)S(1)} %broadcast_compare_fusion.6), kind=kLoop, calls=%fused_computation.17.clone.1 | loop fusion | flops 15722496 | bytes 12633088 | tf_op jit(solution)/shard_map/while/body/eval_jaxpr/reduce_sum | solution.py:164
  211.1 6.2 %bitcast_add_fusion.6 = f32[2,1,256,12,128]{4,2,3,0,1:T(8,128)S(1)} fusion(f32[2,1,256,12,128]{4,2,3,0,1:T(8,128)S(1)} %copy-done.4, f32[2,4,128,256,12]{3,2,4,1,0:T(8,128)S(1)} %get-tuple-element.242, f32[2,256,12]{1,2,0:T(8,128)S(1)} %bitcast.178, pred[2,4,128]{2,1,0:T(4,128)(4,1)S(1)} %broadcast_compare_fusion.6, ...), kind=kOutput, calls=%fused_computation.21.clone.1 | convolution fusion | flops 822607872 | bytes 19204104 | tf_op jit(solution)/shard_map/while/body/eval_jaxpr/rjtgbk,rbjkd->rjtgd/dot_general | solution.py:168
  219.0 3.1 %bitcast_reduce_fusion.2 = (f32[2,256,12]{1,2,0:T(8,128)S(1)}, f32[2,4,128,256,12]{3,2,4,1,0:T(8,128)S(1)}) fusion(pred[2,4,128]{2,1,0:T(4,128)(4,1)S(1)} %broadcast_compare_fusion.6, bf16[2,256,1,12,128]{4,1,3,0,2:T(8,128)(2,1)S(1)} %get-tuple-element.276, bf16[2,32,2,1,128,128]{5,4,2,1,0,3:T(8,128)(2,1)} %get-tuple-element.275, s32[]{:T(128)S(6)} %select_n.274), kind=kOutput, calls=%fused_computation.12.clone.1 | convolution fusion | flops 814737408 | bytes 14443524 | tf_op jit(solution)/shard_map/while/body/eval_jaxpr/rtjgd,rbjkd->rjtgbk/dot_general | solution.py:151
  222.1 3.4 %fusion.94 = f32[2,256,12]{1,2,0:T(8,128)S(1)} fusion(f32[2,4,128,256,12]{3,2,4,1,0:T(8,128)S(1)} %get-tuple-element.242, f32[2,256,12]{1,2,0:T(8,128)S(1)} %bitcast.177, pred[2,4,128]{2,1,0:T(4,128)(4,1)S(1)} %broadcast_compare_fusion.6), kind=kLoop, calls=%fused_computation.17.clone.1 | loop fusion | flops 15722496 | bytes 12633088 | tf_op jit(solution)/shard_map/while/body/eval_jaxpr/reduce_sum | solution.py:164
  225.6 6.2 %bitcast_add_fusion.6 = f32[2,1,256,12,128]{4,2,3,0,1:T(8,128)S(1)} fusion(f32[2,1,256,12,128]{4,2,3,0,1:T(8,128)S(1)} %copy-done.4, f32[2,4,128,256,12]{3,2,4,1,0:T(8,128)S(1)} %get-tuple-element.242, f32[2,256,12]{1,2,0:T(8,128)S(1)} %bitcast.178, pred[2,4,128]{2,1,0:T(4,128)(4,1)S(1)} %broadcast_compare_fusion.6, ...), kind=kOutput, calls=%fused_computation.21.clone.1 | convolution fusion | flops 822607872 | bytes 19204104 | tf_op jit(solution)/shard_map/while/body/eval_jaxpr/rjtgbk,rbjkd->rjtgd/dot_general | solution.py:168
  236.6 3.4 %fusion.94 = f32[2,256,12]{1,2,0:T(8,128)S(1)} fusion(f32[2,4,128,256,12]{3,2,4,1,0:T(8,128)S(1)} %get-tuple-element.242, f32[2,256,12]{1,2,0:T(8,128)S(1)} %bitcast.177, pred[2,4,128]{2,1,0:T(4,128)(4,1)S(1)} %broadcast_compare_fusion.6), kind=kLoop, calls=%fused_computation.17.clone.1 | loop fusion | flops 15722496 | bytes 12633088 | tf_op jit(solution)/shard_map/while/body/eval_jaxpr/reduce_sum | solution.py:164
  240.1 6.2 %bitcast_add_fusion.6 = f32[2,1,256,12,128]{4,2,3,0,1:T(8,128)S(1)} fusion(f32[2,1,256,12,128]{4,2,3,0,1:T(8,128)S(1)} %copy-done.4, f32[2,4,128,256,12]{3,2,4,1,0:T(8,128)S(1)} %get-tuple-element.242, f32[2,256,12]{1,2,0:T(8,128)S(1)} %bitcast.178, pred[2,4,128]{2,1,0:T(4,128)(4,1)S(1)} %broadcast_compare_fusion.6, ...), kind=kOutput, calls=%fused_computation.21.clone.1 | convolution fusion | flops 822607872 | bytes 19204104 | tf_op jit(solution)/shard_map/while/body/eval_jaxpr/rjtgbk,rbjkd->rjtgd/dot_general | solution.py:168
  253.0 3.2 %scatter_fusion = bf16[80,2,128,128]{3,2,1,0:T(8,128)(2,1)} fusion(bf16[80,2,128,128]{3,2,1,0:T(8,128)(2,1)} %bitcast.174, s32[16]{0:T(128)S(1)} %fusion.80, bf16[16,2,128,128]{3,2,1,0:T(8,128)(2,1)S(1)} %bitcast.182), kind=kCustom, calls=%fused_computation.10 | custom fusion | bytes 3145792 | tf_op jit(solution)/shard_map/scatter | solution.py:117
  (181 shorter events, 54.6 us)
Async XLA Ops:
  7.2 9.0 %copy-start = (s32[32,32]{1,0:T(8,128)S(1)}, s32[32,32]{1,0:T(8,128)}, u32[]{:S(2)}) copy-start(s32[32,32]{1,0:T(8,128)} %param.18) | copy-start | bytes 12292
  7.2 7.4 %copy-start.2 = (s32[32]{0:T(128)S(1)}, s32[32]{0:T(128)}, u32[]{:S(2)}) copy-start(s32[32]{0:T(128)} %param.16) | copy-start | bytes 388
  7.2 7.2 %copy-start.9 = (s32[32]{0:T(128)S(1)}, s32[32]{0:T(128)}, u32[]{:S(2)}) copy-start(s32[32]{0:T(128)} %param.17) | copy-start | bytes 388
  7.2 99.5 %all-gather.2.cloned.1.call-start = ((), (), s32[]{:S(2)}) async-start(), calls=%async_computation.2 | async-start | bytes 14155776 | tf_op jit(solution)/shard_map/all_gather | solution.py:71
  14.2 1.3 copy-start.6
  29.7 10.5 %copy-start.3 = (bf16[512,1536]{1,0:T(8,128)(2,1)S(1)}, bf16[512,1536]{1,0:T(8,128)(2,1)}, u32[]{:S(2)}) copy-start(bf16[512,1536]{1,0:T(8,128)(2,1)} %param.13) | copy-start | bytes 4718596
  29.7 15.0 %copy-start.7 = (s32[32,2]{0,1:T(2,128)S(1)}, s32[32,2]{0,1:T(2,128)}, u32[]{:S(2)}) copy-start(s32[32,2]{0,1:T(2,128)} %param.20) | copy-start | bytes 772
  29.7 16.3 %copy-start.8 = (s32[32,2]{0,1:T(2,128)S(1)}, s32[32,2]{0,1:T(2,128)}, u32[]{:S(2)}) copy-start(s32[32,2]{0,1:T(2,128)} %param.21) | copy-start | bytes 772
  29.7 71.7 %all-to-all-start = ((bf16[16,4,2,1,128,128]{5,4,2,1,3,0:T(8,128)(2,1)}), bf16[16,4,2,1,128,128]{5,4,2,1,3,0:T(8,128)(2,1)}, u32[]{:S(2)}, u32[]{:S(2)}) async-start(bf16[16,4,2,1,128,128]{5,4,2,1,3,0:T(8,128)(2,1)} %broadcast_select_fusion), calls=%async_computation | async-start | bytes 8388608 | tf_op jit(solution)/shard_map/all_to_all | solution.py:109
  118.9 134.1 %all-to-all-start.1 = ((bf16[16,1,2,1,128,128]{5,4,3,2,1,0:T(8,128)(2,1)}), bf16[16,1,2,1,128,128]{5,4,3,2,1,0:T(8,128)(2,1)S(1)}, u32[]{:S(2)}, u32[]{:S(2)}) async-start(bf16[16,1,2,1,128,128]{5,4,3,2,1,0:T(8,128)(2,1)} %copy.135), calls=%async_computation.1 | async-start | bytes 2097152 | tf_op jit(solution)/shard_map/all_to_all | solution.py:110
  135.2 3.4 %copy-start.4 = (f32[2,1,256,12,128]{4,2,3,0,1:T(8,128)S(1)}, f32[2,1,256,12,128]{4,2,3,0,1:T(8,128)}, u32[]{:S(2)}) copy-start(f32[2,1,256,12,128]{4,2,3,0,1:T(8,128)} %get-tuple-element.260) | copy-start | bytes 9437188 | tf_op jit(solution)/shard_map/while
  144.8 1.7 copy-start.5
  149.7 3.4 %copy-start.4 = (f32[2,1,256,12,128]{4,2,3,0,1:T(8,128)S(1)}, f32[2,1,256,12,128]{4,2,3,0,1:T(8,128)}, u32[]{:S(2)}) copy-start(f32[2,1,256,12,128]{4,2,3,0,1:T(8,128)} %get-tuple-element.260) | copy-start | bytes 9437188 | tf_op jit(solution)/shard_map/while
  159.3 1.7 copy-start.5
  164.2 3.4 %copy-start.4 = (f32[2,1,256,12,128]{4,2,3,0,1:T(8,128)S(1)}, f32[2,1,256,12,128]{4,2,3,0,1:T(8,128)}, u32[]{:S(2)}) copy-start(f32[2,1,256,12,128]{4,2,3,0,1:T(8,128)} %get-tuple-element.260) | copy-start | bytes 9437188 | tf_op jit(solution)/shard_map/while
  173.8 1.7 copy-start.5
  178.6 3.4 %copy-start.4 = (f32[2,1,256,12,128]{4,2,3,0,1:T(8,128)S(1)}, f32[2,1,256,12,128]{4,2,3,0,1:T(8,128)}, u32[]{:S(2)}) copy-start(f32[2,1,256,12,128]{4,2,3,0,1:T(8,128)} %get-tuple-element.260) | copy-start | bytes 9437188 | tf_op jit(solution)/shard_map/while
  188.3 1.7 copy-start.5
  193.1 3.4 %copy-start.4 = (f32[2,1,256,12,128]{4,2,3,0,1:T(8,128)S(1)}, f32[2,1,256,12,128]{4,2,3,0,1:T(8,128)}, u32[]{:S(2)}) copy-start(f32[2,1,256,12,128]{4,2,3,0,1:T(8,128)} %get-tuple-element.260) | copy-start | bytes 9437188 | tf_op jit(solution)/shard_map/while
  202.8 1.7 copy-start.5
  207.6 3.4 %copy-start.4 = (f32[2,1,256,12,128]{4,2,3,0,1:T(8,128)S(1)}, f32[2,1,256,12,128]{4,2,3,0,1:T(8,128)}, u32[]{:S(2)}) copy-start(f32[2,1,256,12,128]{4,2,3,0,1:T(8,128)} %get-tuple-element.260) | copy-start | bytes 9437188 | tf_op jit(solution)/shard_map/while
  217.3 1.7 copy-start.5
  222.1 3.4 %copy-start.4 = (f32[2,1,256,12,128]{4,2,3,0,1:T(8,128)S(1)}, f32[2,1,256,12,128]{4,2,3,0,1:T(8,128)}, u32[]{:S(2)}) copy-start(f32[2,1,256,12,128]{4,2,3,0,1:T(8,128)} %get-tuple-element.260) | copy-start | bytes 9437188 | tf_op jit(solution)/shard_map/while
  231.8 1.7 copy-start.5
  236.6 3.4 %copy-start.4 = (f32[2,1,256,12,128]{4,2,3,0,1:T(8,128)S(1)}, f32[2,1,256,12,128]{4,2,3,0,1:T(8,128)}, u32[]{:S(2)}) copy-start(f32[2,1,256,12,128]{4,2,3,0,1:T(8,128)} %get-tuple-element.260) | copy-start | bytes 9437188 | tf_op jit(solution)/shard_map/while
  246.3 1.7 copy-start.5
  247.9 8.2 %copy-start.1 = (s32[32,32]{1,0:T(8,128)S(1)}, s32[32,32]{1,0:T(8,128)}, u32[]{:S(2)}) copy-start(s32[32,32]{1,0:T(8,128)} %param.18) | copy-start | bytes 12292
Sparse Core Ops, SparseCore 0:
  14.4 70.9 all-gather.1
where the time goes:
time: 265 us; the launch traced here: 263 us
  matrix products  90.1 us (34%)
  local copies, waits for them, and re-layouts  52.2 us (20%)
  waiting for transfers between devices  49.8 us (19%)
  other arithmetic  42 us (16%)
  between operations  14.4 us (5%)
  starting transfers between devices  13.9 us (5%)
    all_to_all x1, waiting for transfers between devices, per_device(): lax.all_to_all(pull_send, 'grp', split_axis=0, concat_axis=0, tiled=True)  49.8 us
    dot_general x8, matrix products, visit(): jnp.einsum('rjtgbk,rbjkd->rjtgd', block_weights, key_part[:, :, 1], prefe...  49.5 us
    reduce_sum x8, other arithmetic, visit(): running_sum = running_sum * rescale + jnp.sum(block_weights, axis=-1)  27.4 us
    dot_general x8, matrix products, visit(): jnp.einsum('rtjgd,rbjkd->rjtgbk', query_rows, key_part[:, :, 0], preferre...  24.6 us
    while x40, local copies, waits for them, and re-layouts  13 us
    unnamed x21, local copies, waits for them, and re-layouts  9.81 us
    all_to_all x1, starting transfers between devices, per_device(): lax.all_to_all(pull_send, 'grp', split_axis=0, concat_axis=0, tiled=True)  9.18 us
    dot_general x1, matrix products, per_device(): jnp.einsum('td,dcjh->jtch', shard_piece, row_block, preferred_element_typ...  8.33 us
  transfers between devices with their start and end apart: 3, of which 1 were waited for; matrix products, arithmetic and copies ran while one was open for 57% of the time, Pallas kernels for 0%

commit v1 on v0

v1 whole, which is shorter than its diff:
```python
import functools
import math

import jax
import jax.numpy as jnp
from jax import lax
from jax.experimental import pallas as pl
from jax.experimental.pallas import tpu as pltpu
from jax.sharding import PartitionSpec as P

MESH = pl.DeviceIdType.MESH
ROPE_BASE = 1000000.0
MASKED = -1e30
BLK = 128
HD = 128
ROUNDS = 4
PER_ROUND = 8
HEADS_PER_STEP = 6
bf16 = jnp.bfloat16
f32 = jnp.float32


def remote(src, dst, send_sem, recv_sem, device):
    return pltpu.make_async_remote_copy(
        src_ref=src,
        dst_ref=dst,
        send_sem=send_sem,
        recv_sem=recv_sem,
        device_id=device,
        device_id_type=MESH,
    )


def drain(ref, sem):
    pltpu.make_async_copy(ref, ref, sem).wait()


def gather_kernel(rows_ref, pool_ref, out_ref, sem):
    count = out_ref.shape[0]

    def go(i, _):
        pltpu.make_async_copy(pool_ref.at[rows_ref[i]], out_ref.at[i], sem).start()
        return 0

    lax.fori_loop(0, count, go, 0)
    drain(out_ref, sem)


def patch_kernel(rows_ref, pool_ref, pushed_ref, out_ref, sem):
    del pool_ref
    count = pushed_ref.shape[0]
    limit = out_ref.shape[0]

    def go(i, _):
        @pl.when(rows_ref[i] < limit)
        def _():
            pltpu.make_async_copy(pushed_ref.at[i], out_ref.at[rows_ref[i]], sem.at[i]).start()

        return 0

    def done(i, _):
        @pl.when(rows_ref[i] < limit)
        def _():
            pltpu.make_async_copy(pushed_ref.at[i], out_ref.at[rows_ref[i]], sem.at[i]).wait()

        return 0

    lax.fori_loop(0, count, go, 0)
    lax.fori_loop(0, count, done, 0)


def main_kernel(
    tab_ref,
    len_ref,
    pick_ref,
    cos_ref,
    sin_ref,
    hid_ref,
    q_hbm,
    w_ref,
    snd_ref,
    att_ref,
    pushed_ref,
    arr0,
    arr1,
    arr2,
    arr3,
    qv,
    hown,
    hl,
    hr,
    ho,
    wown,
    wsib,
    pown,
    psib,
    pget,
    kc,
    vc,
    m_ref,
    acc_ref,
    nkv,
    pbuf,
    loc_sem,
    ws_sem,
    wr_sem,
    ls_sem,
    lr_sem,
    rs_sem,
    rr_sem,
    fs_sem,
    frl_sem,
    frr_sem,
    as_sem,
    ar_sem,
    xs_sem,
    xr_sem,
    ps_sem,
    pr_sem,
):
    groups = lax.axis_size("grp")
    arrs = (arr0, arr1, arr2, arr3)
    g = lax.axis_index("grp")
    t = lax.axis_index("tp")
    chips = lax.axis_size("tp") // 2
    y = t // 2
    core = t % 2
    right = lax.rem(y + 1, chips) * 2 + core
    left = lax.rem(y + chips - 1, chips) * 2 + core
    sib = y * 2 + 1 - core
    width = hid_ref.shape[1]
    half = width // 2
    pieces = hid_ref.shape[0] // BLK
    heads = q_hbm.shape[1] // HD
    scale = math.log2(math.e) / math.sqrt(HD)

    barrier = pltpu.get_barrier_semaphore()

    def greet(k, _):
        pl.semaphore_signal(
            barrier, inc=1, device_id=(lax.rem(g + k, groups), t), device_id_type=MESH
        )
        return 0

    lax.fori_loop(1, groups, greet, 0)
    for peer in (right, left, sib):
        pl.semaphore_signal(barrier, inc=1, device_id=(g, peer), device_id_type=MESH)
    pl.semaphore_wait(barrier, groups + 2)

    own_right = []
    own_left = []
    for p in range(pieces):
        rows = pl.ds(p * BLK, BLK)
        a = remote(hid_ref.at[rows], hl.at[p], ls_sem.at[p], lr_sem.at[p], (g, right))
        b = remote(hid_ref.at[rows], hr.at[p], rs_sem.at[p], rr_sem.at[p], (g, left))
        a.start()
        b.start()
        own_right.append(a)
        own_left.append(b)

    def send_round(rho):
        def go(k, _):
            d = lax.rem(g + k, groups)
            remote(
                snd_ref.at[rho, d], arrs[rho].at[g], as_sem.at[rho], ar_sem.at[rho], (d, t)
            ).start()
            return 0

        lax.fori_loop(1, groups, go, 0)
        pltpu.make_async_copy(snd_ref.at[rho, g], arrs[rho].at[g], loc_sem.at[rho]).start()

    for rho in range(ROUNDS):
        send_round(rho)

    wcopies = []
    for i in range(chips):
        wcopies.append(
            remote(
                w_ref.at[pl.ds((2 * i + 1 - core) * width, width)],
                wsib.at[i],
                ws_sem.at[i],
                wr_sem.at[i],
                (g, sib),
            )
        )
        wcopies[-1].start()
    local = [
        pltpu.make_async_copy(q_hbm, qv, loc_sem.at[4]),
        pltpu.make_async_copy(hid_ref, hown, loc_sem.at[5]),
    ]
    for i in range(chips):
        local.append(
            pltpu.make_async_copy(
                w_ref.at[pl.ds((2 * i + core) * width, width)], wown.at[i], loc_sem.at[6 + i]
            )
        )
    for c in local:
        c.start()

    m_ref[...] = jnp.full_like(m_ref, MASKED)
    acc_ref[...] = jnp.zeros_like(acc_ref)
    for c in local:
        c.wait()
    for c in wcopies:
        c.wait()

    def project(piece, src, owner, first):
        rows = pl.ds(piece * BLK, BLK)
        x = src
        a = jnp.dot(x, wown[owner], preferred_element_type=f32)
        b = jnp.dot(x, wsib[owner], preferred_element_type=f32)
        if first:
            pown[rows, :] = a
            psib[rows, :] = b
        else:
            pown[rows, :] += a
            psib[rows, :] += b

    def own_piece(p, _):
        project(p, hown[pl.ds(p * BLK, BLK), :], y, True)
        return 0

    lax.fori_loop(0, pieces, own_piece, 0)

    at_left = lax.rem(y + chips - 1, chips)
    at_right = lax.rem(y + 1, chips)
    at_far = lax.rem(y + 2, chips)

    forwards = []
    for rho in range(ROUNDS):
        p = rho
        own_right[p].wait_recv()
        f = remote(
            hl.at[p, :, pl.ds(0, half)],
            ho.at[p, :, pl.ds(0, half)],
            fs_sem.at[p],
            frl_sem.at[p],
            (g, right),
        )
        f.start()
        forwards.append(f)
        own_left[p].wait_recv()
        f = remote(
            hr.at[p, :, pl.ds(half, half)],
            ho.at[p, :, pl.ds(half, half)],
            fs_sem.at[pieces + p],
            frr_sem.at[p],
            (g, left),
        )
        f.start()
        forwards.append(f)

        arr = arrs[rho]
        drain(arr.at[pl.ds(0, groups - 1)], ar_sem.at[rho])
        pltpu.make_async_copy(snd_ref.at[rho, g], arr.at[g], loc_sem.at[rho]).wait()

        def request(r, _, arr=arr, rho=rho):
            limit = len_ref[r]

            def place(i, _):
                code = tab_ref[r, rho * PER_ROUND + i]
                block = code // groups
                holder = code % groups
                rows = pl.ds(pl.multiple_of(i * BLK, BLK), BLK)
                live = (
                    lax.broadcasted_iota(jnp.int32, (BLK, HD), 0) + block * BLK < limit
                )
                kc[rows, 0:HD] = arr[holder, 0]
                kc[rows, HD : 2 * HD] = jnp.where(live, 0.0, MASKED).astype(bf16)
                vc[rows, 0:HD] = jnp.where(live, arr[holder, 1].astype(f32), 0.0).astype(bf16)
                vc[rows, HD : 2 * HD] = jnp.where(live, 1.0, 0.0).astype(bf16)
                return 0

            lax.fori_loop(0, PER_ROUND, place, 0)

            def step(s, _):
                scores = []
                for u in range(HEADS_PER_STEP):
                    h = s * HEADS_PER_STEP + u
                    q = qv[
                        pl.ds(pl.multiple_of(r * 2 * BLK, 2 * BLK), 2 * BLK),
                        pl.ds(pl.multiple_of(h * HD, HD), HD),
                    ]
                    q = jnp.concatenate([q, jnp.ones_like(q)], axis=1)
                    scores.append(
                        lax.dot_general(
                            q, kc[...], (((1,), (1,)), ((), ())), preferred_element_type=f32
                        )
                    )
                for u in range(HEADS_PER_STEP):
                    i = r * heads + s * HEADS_PER_STEP + u
                    old = m_ref[i]
                    new = jnp.maximum(old, jnp.max(scores[u], axis=1, keepdims=True))
                    alpha = jnp.exp2((old - new) * scale)
                    w = jnp.exp2((scores[u] - new[:, :1]) * scale).astype(bf16)
                    o = jnp.dot(w, vc[...], preferred_element_type=f32)
                    m_ref[i] = new
                    acc_ref[i, :, 0:HD] = acc_ref[i, :, 0:HD] * alpha + o[:, :HD]
                    acc_ref[i, :, HD:] = acc_ref[i, :, HD:] * alpha + o[:, HD:]
                return 0

            lax.fori_loop(0, heads // HEADS_PER_STEP, step, 0)
            return 0

        lax.fori_loop(0, 2, request, 0)
        project(p, hl[p], at_left, False)
        project(p, hr[p], at_right, False)

    exchange = []
    for p in range(pieces):
        rows = pl.ds(p * BLK, BLK)
        pltpu.make_async_copy(
            ho.at[p, :, pl.ds(0, half)], ho.at[p, :, pl.ds(0, half)], frl_sem.at[p]
        ).wait()
        pltpu.make_async_copy(
            ho.at[p, :, pl.ds(half, half)], ho.at[p, :, pl.ds(half, half)], frr_sem.at[p]
        ).wait()
        project(p, ho[p], at_far, False)
        x = remote(psib.at[rows], pget.at[rows], xs_sem.at[p], xr_sem.at[p], (g, sib))
        x.start()
        exchange.append(x)
    for p in range(pieces):
        rows = pl.ds(p * BLK, BLK)
        exchange[p].wait_recv()
        kv = pown[rows, :] + pget[rows, :]
        k = kv[:, :HD]
        k = k * cos_ref[rows, :] + pltpu.roll(k, HD // 2, 1) * sin_ref[rows, :]
        nkv[p, 0] = k.astype(bf16)
        nkv[p, 1] = kv[:, HD:].astype(bf16)

    def fill(d, _):
        pbuf[d] = nkv[pick_ref[d]]
        return 0

    lax.fori_loop(0, groups, fill, 0)

    def push(k, _):
        d = lax.rem(g + k, groups)
        remote(pbuf.at[d], pushed_ref.at[g], ps_sem, pr_sem, (d, t)).start()
        return 0

    lax.fori_loop(1, groups, push, 0)
    keep = pltpu.make_async_copy(pbuf.at[g], pushed_ref.at[g], loc_sem.at[10])
    keep.start()

    def fresh_request(r, _):
        kn = jnp.concatenate([nkv[2 * r, 0], nkv[2 * r + 1, 0]], axis=0)
        vn = jnp.concatenate([nkv[2 * r, 1], nkv[2 * r + 1, 1]], axis=0)
        vn = jnp.concatenate([vn, jnp.ones_like(vn)], axis=1)
        causal = lax.broadcasted_iota(jnp.int32, (2 * BLK, 2 * BLK), 1) <= (
            lax.broadcasted_iota(jnp.int32, (2 * BLK, 2 * BLK), 0)
        )

        def step(s, _):
            scores = []
            for u in range(HEADS_PER_STEP):
                h = s * HEADS_PER_STEP + u
                q = qv[
                    pl.ds(pl.multiple_of(r * 2 * BLK, 2 * BLK), 2 * BLK),
                    pl.ds(pl.multiple_of(h * HD, HD), HD),
                ]
                sc = lax.dot_general(
                    q, kn, (((1,), (1,)), ((), ())), preferred_element_type=f32
                )
                scores.append(jnp.where(causal, sc, MASKED))
            for u in range(HEADS_PER_STEP):
                h = s * HEADS_PER_STEP + u
                i = r * heads + h
                old = m_ref[i]
                new = jnp.maximum(old, jnp.max(scores[u], axis=1, keepdims=True))
                alpha = jnp.exp2((old - new) * scale)
                w = jnp.exp2((scores[u] - new[:, :1]) * scale).astype(bf16)
                o = jnp.dot(w, vn, preferred_element_type=f32)
                total = acc_ref[i, :, HD:] * alpha + o[:, HD:]
                value = acc_ref[i, :, 0:HD] * alpha + o[:, :HD]
                att_ref[
                    pl.ds(pl.multiple_of(r * 2 * BLK, 2 * BLK), 2 * BLK),
                    pl.ds(pl.multiple_of(h * HD, HD), HD),
                ] = (value / total).astype(bf16)
            return 0

        lax.fori_loop(0, heads // HEADS_PER_STEP, step, 0)
        return 0

    lax.fori_loop(0, 2, fresh_request, 0)

    for p in range(pieces):
        own_right[p].wait_send()
        own_left[p].wait_send()
        exchange[p].wait_send()
    for f in forwards:
        f.wait_send()
    for rho in range(ROUNDS):
        drain(snd_ref.at[rho, pl.ds(0, groups - 1)], as_sem.at[rho])
    keep.wait()
    drain(pbuf.at[pl.ds(0, groups - 1)], ps_sem)
    drain(pushed_ref.at[pl.ds(0, groups - 1)], pr_sem)


def tables(hit_holder, hit_slot, order, me, groups):
    holder = hit_holder[order].reshape(groups, 2, -1)
    slot = hit_slot[order].reshape(groups, 2, -1)
    count = holder.shape[2]
    h0 = holder[:, 0]
    earlier = jnp.arange(count)[None, :] < jnp.arange(count)[:, None]
    rank = jnp.sum(
        (holder[:, :, :, None] == holder[:, :, None, :]) & earlier[None, None], axis=-1, dtype=jnp.int32
    )
    below = jnp.sum(h0[:, None, None, :] < holder[:, :, :, None], axis=-1, dtype=jnp.int32)
    upto = jnp.sum(h0[:, None, None, :] <= holder[:, :, :, None], axis=-1, dtype=jnp.int32)
    first = (jnp.arange(2) == 0)[None, :, None]
    index = jnp.where(first, below, upto) + rank
    turn = index & 3
    place = jnp.where(first, index >> 2, holder - ((below + 3 - turn) >> 2))
    mine = (holder == me)[None] & (turn[None] == jnp.arange(ROUNDS)[:, None, None, None])
    send_rows = jnp.sum(jnp.where(mine, slot[None], 0), axis=(2, 3))
    flat = turn * PER_ROUND + place
    code = jnp.arange(count, dtype=jnp.int32) * groups + holder
    my_flat = lax.dynamic_index_in_dim(flat, me, 0, False)
    my_code = lax.dynamic_index_in_dim(code, me, 0, False)
    hit = my_flat[:, None, :] == jnp.arange(count)[None, :, None]
    table = jnp.sum(jnp.where(hit, my_code[:, None, :], 0), axis=-1)
    return send_rows.astype(jnp.int32), table.astype(jnp.int32)


def per_device(
    hidden,
    queries,
    keyval_weight,
    keyval_pool,
    prefix_len,
    slot_request,
    hit_holder,
    hit_slot,
    new_owner,
    new_slot,
):
    groups = lax.axis_size("grp")
    me = lax.axis_index("grp")
    rows, width = hidden.shape
    chips = lax.axis_size("tp") // 2
    pieces = rows // BLK
    heads = queries.shape[1] // HD
    pool_slots = keyval_pool.shape[0]
    pool = keyval_pool.reshape(pool_slots, 2, BLK, HD)
    weight = keyval_weight.reshape(-1, 2 * HD)

    my_requests = lax.dynamic_slice_in_dim(slot_request, me * 2, 2)
    lengths = prefix_len[my_requests]
    send_rows, table = tables(hit_holder, hit_slot, slot_request, me, groups)

    token = jnp.arange(rows, dtype=jnp.int32)
    positions = lengths[token // (rows // 2)] + token % (rows // 2)
    frequency = ROPE_BASE ** (-(jnp.arange(HD // 2, dtype=f32) * 2.0 / HD))
    angles = positions.astype(f32)[:, None] * frequency[None, :]
    cosine, sine = jnp.cos(angles), jnp.sin(angles)
    cosine = jnp.concatenate([cosine, cosine], axis=1)
    sine = jnp.concatenate([-sine, sine], axis=1)

    my_owner = new_owner[my_requests].reshape(-1)
    pick = jnp.sum(
        jnp.where(
            my_owner[None, :] == jnp.arange(groups)[:, None],
            jnp.arange(my_owner.shape[0], dtype=jnp.int32)[None, :],
            0,
        ),
        axis=1,
    ).astype(jnp.int32)
    all_owner = new_owner[slot_request].reshape(groups, -1)
    all_slot = new_slot[slot_request].reshape(groups, -1)
    owned = all_owner == me
    target = jnp.where(
        jnp.any(owned, axis=1), jnp.sum(jnp.where(owned, all_slot, 0), axis=1), pool_slots
    ).astype(jnp.int32)

    smem = pl.BlockSpec(memory_space=pltpu.SMEM)
    vmem = pl.BlockSpec(memory_space=pltpu.VMEM)
    anym = pl.BlockSpec(memory_space=pl.ANY)
    dma = pltpu.SemaphoreType.DMA
    V = pltpu.VMEM

    send = pl.pallas_call(
        gather_kernel,
        out_shape=jax.ShapeDtypeStruct((ROUNDS * groups, 2, BLK, HD), bf16),
        in_specs=[smem, anym],
        out_specs=anym,
        scratch_shapes=[dma],
    )(send_rows.reshape(-1), pool)
    send = send.reshape(ROUNDS, groups, 2, BLK, HD)

    attention, pushed = pl.pallas_call(
        main_kernel,
        out_shape=(
            jax.ShapeDtypeStruct(queries.shape, bf16),
            jax.ShapeDtypeStruct((groups, 2, BLK, HD), bf16),
        ),
        in_specs=[smem, smem, smem, vmem, vmem, anym, anym, anym, anym],
        out_specs=(vmem, anym),
        scratch_shapes=[V((groups, 2, BLK, HD), bf16)] * ROUNDS
        + [
            V(queries.shape, bf16),
            V((rows, width), bf16),
            V((pieces, BLK, width), bf16),
            V((pieces, BLK, width), bf16),
            V((pieces, BLK, width), bf16),
            V((chips, width, 2 * HD), bf16),
            V((chips, width, 2 * HD), bf16),
            V((rows, 2 * HD), f32),
            V((rows, 2 * HD), f32),
            V((rows, 2 * HD), f32),
            V((PER_ROUND * BLK, 2 * HD), bf16),
            V((PER_ROUND * BLK, 2 * HD), bf16),
            V((2 * heads, 2 * BLK, HD), f32),
            V((2 * heads, 2 * BLK, 2 * HD), f32),
            V((pieces, 2, BLK, HD), bf16),
            V((groups, 2, BLK, HD), bf16),
            dma((11,)),
            dma((chips,)),
            dma((chips,)),
            dma((pieces,)),
            dma((pieces,)),
            dma((pieces,)),
            dma((pieces,)),
            dma((2 * pieces,)),
            dma((pieces,)),
            dma((pieces,)),
            dma((ROUNDS,)),
            dma((ROUNDS,)),
            dma((pieces,)),
            dma((pieces,)),
            dma,
            dma,
        ],
        compiler_params=pltpu.CompilerParams(
            collective_id=0, has_side_effects=True, vmem_limit_bytes=60 * 2**20
        ),
    )(table, lengths, pick, cosine, sine, hidden, queries, weight, send)

    new_pool = pl.pallas_call(
        patch_kernel,
        out_shape=jax.ShapeDtypeStruct(pool.shape, bf16),
        in_specs=[smem, anym, anym],
        out_specs=anym,
        scratch_shapes=[dma((groups,))],
        input_output_aliases={1: 0},
    )(target, pool, pushed)
    return attention, new_pool.reshape(keyval_pool.shape)


def solution(mesh):
    in_specs = (
        P("grp", "tp"),
        P("grp", "tp"),
        P(None, None, "tp"),
        P("grp", None, "tp", None, None),
        P(),
        P(),
        P(),
        P(),
        P(),
        P(),
    )
    out_specs = (P("grp", "tp"), P("grp", None, "tp", None, None))
    return jax.shard_map(
        per_device, mesh=mesh, in_specs=in_specs, out_specs=out_specs, check_vma=False
    )
```

time: 265 us -> 266 us (level)
  Pallas kernels: 0 us -> 236 us
  matrix products: 90.1 us -> 0 us
  waiting for transfers between devices: 49.8 us -> 0 us
  other arithmetic: 42 us -> 8.08 us
  local copies, waits for them, and re-layouts: 52.2 us -> 21.2 us
  starting transfers between devices: 13.9 us -> 0 us
  between operations: 14.4 us -> 0.87 us
    pallas_call x0 -> x3, Pallas kernels: none -> 236 us  [the longest x1 129 us: per_device(): pl.pallas_call(gather_kernel, out_shape=jax.ShapeDtypeStruct((ROUNDS * gr...]
    dot_general x21 -> x0, matrix products: 90.1 us -> none  [the longest x8 49.5 us: visit(): jnp.einsum('rjtgbk,rbjkd->rjtgd', block_weights, key_part[:, :, 1], prefe...]
    all_to_all x2 -> x0, waiting for transfers between devices: 49.8 us -> none  [the longest x1 49.8 us: per_device(): lax.all_to_all(pull_send, 'grp', split_axis=0, concat_axis=0, tiled=True)]
    reduce_sum x11 -> x4, other arithmetic: 29.3 us -> 3.44 us  [the longest x1 1.95 us: tables(): jnp.sum(h0[:, None, None, :] <= holder[:, :, :, None], axis=-1, dtype=jnp...]
    while x41 -> x0, local copies, waits for them, and re-layouts: 15 us -> none
    all_to_all x2 -> x0, starting transfers between devices: 13.8 us -> none  [the longest x1 9.18 us: per_device(): lax.all_to_all(pull_send, 'grp', split_axis=0, concat_axis=0, tiled=True)]
    gather x10 -> x5, local copies, waits for them, and re-layouts: 15 us -> 2.94 us  [the longest x1 0.64 us: per_device(): lengths = prefix_len[my_requests]]
    unnamed x21, local copies, waits for them, and re-layouts: 9.81 us -> 16.2 us
  transfers between devices with their start and end apart: 3 -> 0, of which waited for: 1 -> 0; matrix products, arithmetic and copies ran while one was open for 57% -> 0% of each run, Pallas kernels for 0% -> 0%
where the time goes in v1:
time: 266 us
  Pallas kernels  236 us (89%)
  local copies, waits for them, and re-layouts  21.2 us (8%)
  other arithmetic  8.08 us (3%)
    pallas_call x1, Pallas kernels, per_device(): pl.pallas_call(gather_kernel, out_shape=jax.ShapeDtypeStruct((ROUNDS * gr...  129 us
    pallas_call x1, Pallas kernels, per_device(): pl.pallas_call(main_kernel, out_shape=(jax.ShapeDtypeStruct(queries.shape...  94.8 us
    unnamed x21, local copies, waits for them, and re-layouts  16.2 us
    pallas_call x1, Pallas kernels, per_device(): pl.pallas_call(patch_kernel, out_shape=jax.ShapeDtypeStruct(pool.shape, b...  12 us

profile of v1, /device:TPU:1, one launch (start us, length us, event | category | flops | bytes accessed | tf_op | source)
XLA Modules:
  0.0 265.9 jit_solution(578970686386406553)
XLA Ops:
  0.7 7.0 %copy.34 = bf16[80,2,1,128,128]{4,3,2,1,0:T(8,128)(2,1)} copy(bf16[80,2,1,128,128]{4,3,2,1,0:T(8,128)(2,1)} %param.13) | data formatting | bytes 10485760
  7.8 0.6 gather_fusion.1
  8.5 0.6 fusion.13
  9.1 1.3 compare_select_fusion.1
  10.5 0.1 copy.21
  10.6 0.6 gather_fusion.2
  11.1 0.1 eq.90
  11.2 0.6 select_reduce_fusion.3.pick_ref
  11.8 0.6 gather_fusion.4
  12.4 0.6 gather_fusion.3
  13.0 0.6 gather_fusion
  13.6 0.1 copy.26
  13.7 0.6 gather_fusion.5
  14.3 0.1 select_reduce_fusion.2
  14.4 0.1 reduce_or.10
  14.5 0.1 reduce_or.14
  14.6 0.1 reduce_or.18
  14.8 0.1 reduce_sum.77
  14.8 0.1 reduce_sum.78
  15.0 0.5 broadcast_select_fusion.rows_ref
  15.5 1.9 convert_reduce_fusion.1
  17.4 0.1 broadcast_and_fusion
  17.6 0.2 select_reduce_fusion
  17.8 0.7 reshape.133.rows_ref
  18.4 0.7 select_reduce_fusion.1.tab_ref
  19.1 1.0 fusion
  20.1 1.0 pad_maximum_fusion
  21.1 129.0 %shard_map.113 = bf16[64,2,128,128]{3,2,1,0:T(8,128)(2,1)} custom-call(s32[64]{0:T(128)} %reshape.133.rows_ref, bf16[80,2,128,128]{3,2,1,0:T(8,128)(2,1)} %bitcast.19), custom_call_target="tpu_custom_call" | custom-call | tf_op jit(solution)/shard_map/pallas_call | solution.py:482
  150.2 7.8 %copy.30 = bf16[1536,8,2,128]{3,1,2,0:T(8,128)(2,1)} copy(bf16[1536,8,2,128]{3,2,1,0:T(2,128)(2,1)} %bitcast.24) | data formatting | bytes 12582912
  158.0 94.8 %shard_map.114 = (bf16[512,1536]{1,0:T(8,128)(2,1)}, bf16[16,2,128,128]{3,2,1,0:T(8,128)(2,1)}) custom-call(s32[2,32]{1,0:T(2,128)} %select_reduce_fusion.1.tab_ref, s32[2]{0:T(128)} %copy-done.4, s32[16]{0:T(128)} %select_reduce_fusion.3.pick_ref, f32[512,128]{1,0:T(8,128)} %get-tuple-element.26.cos_ref, f32[512,128]{1,0:T(8,128)} %get-tuple-element.27.sin_ref, ...), custom_call_target="tpu_custom_call" | custom-call | tf_op jit(solution)/shard_map/pallas_call | solution.py:491
  252.8 12.0 %shard_map.115 = bf16[80,2,128,128]{3,2,1,0:T(8,128)(2,1)} custom-call(s32[16]{0:T(128)} %broadcast_select_fusion.rows_ref, bf16[80,2,128,128]{3,2,1,0:T(8,128)(2,1)} %bitcast.20, bf16[16,2,128,128]{3,2,1,0:T(8,128)(2,1)} %get-tuple-element.5.pushed_ref), custom_call_target="tpu_custom_call", output_to_operand_aliasing={{}: (1, {})} | custom-call | tf_op jit(solution)/shard_map/pallas_call | solution.py:539
  264.8 1.1 copy.35
  (31 shorter events, 0.3 us)
Async XLA Ops:
  0.6 11.8 %copy-start = (s32[32,32]{1,0:T(8,128)S(1)}, s32[32,32]{1,0:T(8,128)}, u32[]{:S(2)}) copy-start(s32[32,32]{1,0:T(8,128)} %param.17) | copy-start | bytes 12292
  0.6 7.2 %copy-start.1 = (s32[32]{0:T(128)S(1)}, s32[32]{0:T(128)}, u32[]{:S(2)}) copy-start(s32[32]{0:T(128)} %param.14) | copy-start | bytes 388
  0.7 7.0 %copy-start.7 = (s32[32]{0:T(128)S(1)}, s32[32]{0:T(128)}, u32[]{:S(2)}) copy-start(s32[32]{0:T(128)} %param.15) | copy-start | bytes 388
  0.7 12.3 %copy-start.3 = (s32[32,32]{1,0:T(8,128)S(1)}, s32[32,32]{1,0:T(8,128)}, u32[]{:S(2)}) copy-start(s32[32,32]{1,0:T(8,128)} %param.16) | copy-start | bytes 12292
  0.7 9.8 %copy-start.5 = (s32[32,2]{0,1:T(2,128)S(1)}, s32[32,2]{0,1:T(2,128)}, u32[]{:S(2)}) copy-start(s32[32,2]{0,1:T(2,128)} %param.18) | copy-start | bytes 772
  0.7 13.0 %copy-start.6 = (s32[32,2]{0,1:T(2,128)S(1)}, s32[32,2]{0,1:T(2,128)}, u32[]{:S(2)}) copy-start(s32[32,2]{0,1:T(2,128)} %param.19) | copy-start | bytes 772
  8.5 141.7 %copy-start.4 = (s32[2]{0:T(128)}, s32[2]{0:T(128)S(1)}, u32[]{:S(2)}) copy-start(s32[2]{0:T(128)S(1)} %gather_fusion.1) | copy-start | bytes 28
  252.8 12.0 %copy-start.2 = (bf16[512,1536]{1,0:T(8,128)(2,1)S(1)}, bf16[512,1536]{1,0:T(8,128)(2,1)}, u32[]{:S(2)}) copy-start(bf16[512,1536]{1,0:T(8,128)(2,1)} %get-tuple-element.30) | copy-start | bytes 4718596

commit v2 on v1

v2 whole, which is shorter than its diff:
```python
import functools
import math

import jax
import jax.numpy as jnp
import numpy as np
from jax import lax
from jax.experimental import pallas as pl
from jax.experimental.pallas import tpu as pltpu
from jax.sharding import PartitionSpec as P

MESH = pl.DeviceIdType.MESH
ROPE_BASE = 1000000.0
MASKED = -1e30
BLK = 128
HD = 128
ROUNDS = 4
PER_ROUND = 8
HEADS_PER_STEP = 6
MAXB = 32
WIDE = 512
bf16 = jnp.bfloat16
f32 = jnp.float32


def remote(src, dst, send_sem, recv_sem, device):
    return pltpu.make_async_remote_copy(
        src_ref=src,
        dst_ref=dst,
        send_sem=send_sem,
        recv_sem=recv_sem,
        device_id=device,
        device_id_type=MESH,
    )


def drain(ref, sem):
    pltpu.make_async_copy(ref, ref, sem).wait()


def store_kernel(
    request_ref, owner_ref, slot_ref, pool_ref, pushed_ref, out_ref, pool, pushed, in_sem, out_sem, push_sem, row_sem
):
    count = pushed_ref.shape[0]
    limit = out_ref.shape[0]
    parts = in_sem.shape[0]
    size = limit // parts
    me = lax.axis_index("grp")
    loads = [
        pltpu.make_async_copy(
            pool_ref.at[pl.ds(i * size, size)], pool.at[pl.ds(i * size, size)], in_sem.at[i]
        )
        for i in range(parts)
    ]
    stores = [
        pltpu.make_async_copy(
            pool.at[pl.ds(i * size, size)], out_ref.at[pl.ds(i * size, size)], out_sem.at[i]
        )
        for i in range(parts)
    ]
    fetch = pltpu.make_async_copy(pushed_ref, pushed, push_sem)
    for c in loads:
        c.start()
    fetch.start()

    def target(i):
        row = limit
        for r in range(2):
            n = request_ref[2 * i + r]
            for c in range(2):
                row = jnp.where(owner_ref[c, n] == me, slot_ref[c, n], row)
        return row

    for i in range(parts):
        loads[i].wait()
        stores[i].start()
    fetch.wait()
    for c in stores:
        c.wait()

    def go(i, _):
        row = target(i)

        @pl.when(row < limit)
        def _():
            pltpu.make_async_copy(pushed.at[i], out_ref.at[row], row_sem.at[i]).start()

        return 0

    def done(i, _):
        row = target(i)

        @pl.when(row < limit)
        def _():
            pltpu.make_async_copy(pushed.at[i], out_ref.at[row], row_sem.at[i]).wait()

        return 0

    lax.fori_loop(0, count, go, 0)
    lax.fori_loop(0, count, done, 0)


def running_count(marks):
    lane = lax.broadcasted_iota(jnp.int32, marks.shape, 1)
    total = marks
    for shift in (1, 2, 4, 8, 16):
        total = total + jnp.where(lane >= shift, pltpu.roll(total, shift, 1), 0)
    return total - marks


def rows_to_send(h0, h1, s0, s1, me):
    e0 = (h0 == me).astype(jnp.int32)
    e1 = (h1 == me).astype(jnp.int32)
    start = jnp.sum(((h0 >= 0) & (h0 < me)).astype(jnp.int32), axis=1, keepdims=True)
    mine = jnp.sum(e0, axis=1, keepdims=True)
    turn0 = (running_count(e0) + start) & (ROUNDS - 1)
    turn1 = (running_count(e1) + (start + mine)) & (ROUNDS - 1)
    lane = lax.broadcasted_iota(jnp.int32, h0.shape, 1)
    rows = jnp.zeros_like(h0)
    for rho in range(ROUNDS):
        chosen = jnp.where((e0 == 1) & (turn0 == rho), s0, 0) + jnp.where(
            (e1 == 1) & (turn1 == rho), s1, 0
        )
        rows = jnp.where(lane == rho, jnp.sum(chosen, axis=1, keepdims=True), rows)
    return rows


def blocks_to_read(h0, h1, groups):
    count = MAXB
    sub = lax.broadcasted_iota(jnp.int32, (count, HD), 0)
    lane = lax.broadcasted_iota(jnp.int32, (count, HD), 1)
    inside = lane < count
    eye = sub == lane
    h0 = jnp.broadcast_to(h0, (count, HD))
    h1 = jnp.broadcast_to(h1, (count, HD))
    h0_col = jnp.sum(jnp.where(eye, h0, 0), axis=1, keepdims=True)
    h1_col = jnp.sum(jnp.where(eye, h1, 0), axis=1, keepdims=True)

    def over_rows(mark):
        return jnp.sum(mark.astype(jnp.int32), axis=0, keepdims=True)

    rank0 = over_rows((h0_col == h0) & (sub < lane))
    rank1 = over_rows((h1_col == h1) & (sub < lane))
    below0 = over_rows(h0_col < h0)
    below1 = over_rows(h0_col < h1)
    upto1 = over_rows(h0_col <= h1)
    index0 = below0 + rank0
    place0 = (index0 & (ROUNDS - 1)) * PER_ROUND + (index0 >> 2)
    turn1 = (upto1 + rank1) & (ROUNDS - 1)
    place1 = turn1 * PER_ROUND + h1[0:1] - ((below1 + (ROUNDS - 1) - turn1) >> 2)
    code0 = lane * groups + h0
    code1 = lane * groups + h1
    col0 = jnp.sum(jnp.where((place0 == sub) & inside, code0, 0), axis=1, keepdims=True)
    col1 = jnp.sum(jnp.where((place1 == sub) & inside, code1, 0), axis=1, keepdims=True)
    return jnp.where(lane == 0, col0, jnp.where(lane == 1, col1, 0))


def main_kernel(
    request_ref,
    length_ref,
    owner_ref,
    freq_ref,
    holder_ref,
    slot_ref,
    hid_ref,
    q_hbm,
    w_ref,
    pool_ref,
    att_ref,
    pushed_ref,
    arr0,
    arr1,
    arr2,
    arr3,
    pool,
    sbuf,
    hs,
    tab_v,
    tab,
    qv,
    hown,
    hl,
    hr,
    ho,
    wraw_own,
    wraw_sib,
    wide,
    wown,
    wsib,
    pown,
    psib,
    pget,
    kc,
    vc,
    m_ref,
    acc_ref,
    nkv,
    pbuf,
    loc_sem,
    ws_sem,
    wr_sem,
    ls_sem,
    lr_sem,
    rs_sem,
    rr_sem,
    fs_sem,
    frl_sem,
    frr_sem,
    as_sem,
    ar_sem,
    xs_sem,
    xr_sem,
    ps_sem,
    pr_sem,
):
    groups = lax.axis_size("grp")
    arrs = (arr0, arr1, arr2, arr3)
    g = lax.axis_index("grp")
    t = lax.axis_index("tp")
    chips = lax.axis_size("tp") // 2
    y = t // 2
    core = t % 2
    right = lax.rem(y + 1, chips) * 2 + core
    left = lax.rem(y + chips - 1, chips) * 2 + core
    sib = y * 2 + 1 - core
    width = hid_ref.shape[1]
    half = width // 2
    pieces = hid_ref.shape[0] // BLK
    heads = q_hbm.shape[1] // HD
    scale = math.log2(math.e) / math.sqrt(HD)

    local = [
        pltpu.make_async_copy(pool_ref, pool, loc_sem.at[0]),
        pltpu.make_async_copy(hid_ref, hown, loc_sem.at[1]),
        pltpu.make_async_copy(q_hbm, qv, loc_sem.at[2]),
    ]
    for i in range(chips):
        local.append(
            pltpu.make_async_copy(
                w_ref.at[pl.ds((2 * i + core) * (2 * width), 2 * width)],
                wraw_own.at[i],
                loc_sem.at[3 + i],
            )
        )
    for c in local:
        c.start()

    barrier = pltpu.get_barrier_semaphore()

    def greet(k, _):
        pl.semaphore_signal(
            barrier, inc=1, device_id=(lax.rem(g + k, groups), t), device_id_type=MESH
        )
        return 0

    lax.fori_loop(1, groups, greet, 0)
    for peer in (right, left, sib):
        pl.semaphore_signal(barrier, inc=1, device_id=(g, peer), device_id_type=MESH)
    pl.semaphore_wait(barrier, groups + 2)

    own_right = []
    own_left = []
    for p in range(pieces):
        rows = pl.ds(p * BLK, BLK)
        a = remote(hid_ref.at[rows], hl.at[p], ls_sem.at[p], lr_sem.at[p], (g, right))
        b = remote(hid_ref.at[rows], hr.at[p], rs_sem.at[p], rr_sem.at[p], (g, left))
        a.start()
        b.start()
        own_right.append(a)
        own_left.append(b)

    wcopies = []
    for i in range(chips):
        wcopies.append(
            remote(
                w_ref.at[pl.ds((2 * i + 1 - core) * (2 * width), 2 * width)],
                wraw_sib.at[i],
                ws_sem.at[i],
                wr_sem.at[i],
                (g, sib),
            )
        )
        wcopies[-1].start()

    hs[...] = jnp.full_like(hs, -1)

    def in_order(i, _):
        for r in range(2):
            n = request_ref[2 * i + r]
            hs[r, pl.ds(i, 1), 0:MAXB] = holder_ref[pl.ds(n, 1), :]
            hs[2 + r, pl.ds(i, 1), 0:MAXB] = slot_ref[pl.ds(n, 1), :]
        return 0

    lax.fori_loop(0, groups, in_order, 0)
    tab_v[0:groups] = rows_to_send(hs[0], hs[1], hs[2], hs[3], g)
    tab_v[groups:] = blocks_to_read(hs[0, pl.ds(g, 1), :], hs[1, pl.ds(g, 1), :], groups)
    to_smem = pltpu.make_async_copy(tab_v, tab, loc_sem.at[3 + chips])
    to_smem.start()
    to_smem.wait()
    n0 = request_ref[2 * g]
    n1 = request_ref[2 * g + 1]
    len0 = length_ref[n0]
    len1 = length_ref[n1]

    local[0].wait()
    for rho in range(ROUNDS):
        arr = arrs[rho]

        def fill(k, _, rho=rho, arr=arr):
            d = lax.rem(g + k, groups)
            sbuf[rho, d] = pool[tab[d, rho]]
            remote(sbuf.at[rho, d], arr.at[g], as_sem.at[rho], ar_sem.at[rho], (d, t)).start()
            return 0

        lax.fori_loop(1, groups, fill, 0)
        arr[g] = pool[tab[g, rho]]

    m_ref[...] = jnp.full_like(m_ref, MASKED)
    acc_ref[...] = jnp.zeros_like(acc_ref)

    def unpack(raw, out, i):
        part = WIDE

        def go(j, _):
            wide[0:part] = raw[i, pl.ds(pl.multiple_of(j * part, part), part), :].astype(f32)
            rows = pl.ds(pl.multiple_of(j * (part // 2), part // 2), part // 2)
            out[i, rows, 0:HD] = wide[pl.ds(0, part // 2, stride=2), :].astype(bf16)
            out[i, rows, HD:] = wide[pl.ds(1, part // 2, stride=2), :].astype(bf16)
            return 0

        lax.fori_loop(0, 2 * width // part, go, 0)

    def project(piece, x, owner, first):
        rows = pl.ds(piece * BLK, BLK)
        a = jnp.dot(x, wown[owner], preferred_element_type=f32)
        b = jnp.dot(x, wsib[owner], preferred_element_type=f32)
        if first:
            pown[rows, :] = a
            psib[rows, :] = b
        else:
            pown[rows, :] += a
            psib[rows, :] += b

    at_left = lax.rem(y + chips - 1, chips)
    at_right = lax.rem(y + 1, chips)
    at_far = lax.rem(y + 2, chips)
    forwards = []

    def forward(p):
        own_right[p].wait_recv()
        f = remote(
            hl.at[p, :, pl.ds(0, half)],
            ho.at[p, :, pl.ds(0, half)],
            fs_sem.at[p],
            frl_sem.at[p],
            (g, right),
        )
        f.start()
        forwards.append(f)
        own_left[p].wait_recv()
        f = remote(
            hr.at[p, :, pl.ds(half, half)],
            ho.at[p, :, pl.ds(half, half)],
            fs_sem.at[pieces + p],
            frr_sem.at[p],
            (g, left),
        )
        f.start()
        forwards.append(f)

    def far(p):
        for cols, sem in ((pl.ds(0, half), frl_sem), (pl.ds(half, half), frr_sem)):
            pltpu.make_async_copy(ho.at[p, :, cols], ho.at[p, :, cols], sem.at[p]).wait()
        project(p, ho[p], at_far, False)

    def attend(rho, r):
        arr = arrs[rho]
        limit = (len0, len1)[r]

        def place(i, _):
            code = tab[groups + rho * PER_ROUND + i, r]
            block = code // groups
            holder = code % groups
            rows = pl.ds(pl.multiple_of(i * BLK, BLK), BLK)
            live = lax.broadcasted_iota(jnp.int32, (BLK, HD), 0) + block * BLK < limit
            kc[rows, 0:HD] = arr[holder, 0]
            kc[rows, HD : 2 * HD] = jnp.where(live, 0.0, MASKED).astype(bf16)
            vc[rows, 0:HD] = jnp.where(live, arr[holder, 1].astype(f32), 0.0).astype(bf16)
            vc[rows, HD : 2 * HD] = jnp.where(live, 1.0, 0.0).astype(bf16)
            return 0

        lax.fori_loop(0, PER_ROUND, place, 0)

        def step(s, _):
            scores = []
            for u in range(HEADS_PER_STEP):
                h = s * HEADS_PER_STEP + u
                q = qv[r * 2 * BLK : (r + 1) * 2 * BLK, pl.ds(pl.multiple_of(h * HD, HD), HD)]
                q = jnp.concatenate([q, jnp.ones_like(q)], axis=1)
                scores.append(
                    lax.dot_general(
                        q, kc[...], (((1,), (1,)), ((), ())), preferred_element_type=f32
                    )
                )
            for u in range(HEADS_PER_STEP):
                i = r * heads + s * HEADS_PER_STEP + u
                old = m_ref[i]
                new = jnp.maximum(old, jnp.max(scores[u], axis=1, keepdims=True))
                alpha = jnp.exp2((old - new) * scale)
                w = jnp.exp2((scores[u] - new[:, :1]) * scale).astype(bf16)
                o = jnp.dot(w, vc[...], preferred_element_type=f32)
                m_ref[i] = new
                acc_ref[i, :, 0:HD] = acc_ref[i, :, 0:HD] * alpha + o[:, :HD]
                acc_ref[i, :, HD:] = acc_ref[i, :, HD:] * alpha + o[:, HD:]
            return 0

        lax.fori_loop(0, heads // HEADS_PER_STEP, step, 0)

    def arrived(rho):
        drain(arrs[rho].at[pl.ds(0, groups - 1)], ar_sem.at[rho])

    for c in local[3:]:
        c.wait()

    def own_weights(i, _):
        unpack(wraw_own, wown, i)
        return 0

    lax.fori_loop(0, chips, own_weights, 0)
    local[1].wait()
    local[2].wait()
    forward(0)
    for c in wcopies:
        c.wait()

    def swapped_weights(i, _):
        unpack(wraw_sib, wsib, i)
        return 0

    lax.fori_loop(0, chips, swapped_weights, 0)

    arrived(0)
    attend(0, 0)
    forward(1)
    attend(0, 1)

    def own_piece(p, _):
        project(p, hown[pl.ds(p * BLK, BLK), :], y, True)
        return 0

    lax.fori_loop(0, pieces, own_piece, 0)
    project(0, hl[0], at_left, False)
    project(0, hr[0], at_right, False)
    forward(2)
    arrived(1)
    attend(1, 0)
    project(1, hl[1], at_left, False)
    project(1, hr[1], at_right, False)
    forward(3)
    attend(1, 1)
    for p in (2, 3):
        project(p, hl[p], at_left, False)
        project(p, hr[p], at_right, False)
    arrived(2)
    attend(2, 0)
    attend(2, 1)

    exchange = []
    for p in range(pieces):
        rows = pl.ds(p * BLK, BLK)
        far(p)
        x = remote(psib.at[rows], pget.at[rows], xs_sem.at[p], xr_sem.at[p], (g, sib))
        x.start()
        exchange.append(x)

    row = lax.broadcasted_iota(jnp.int32, (BLK, HD), 0)
    lane = lax.broadcasted_iota(jnp.int32, (BLK, HD), 1)
    for p in range(pieces):
        rows = pl.ds(p * BLK, BLK)
        angle = (row + ((len0, len1)[p // 2] + (p % 2) * BLK)).astype(f32) * freq_ref[...]
        cosine = jnp.cos(angle)
        sine = jnp.where(lane < HD // 2, -1.0, 1.0) * jnp.sin(angle)
        exchange[p].wait_recv()
        kv = pown[rows, :] + pget[rows, :]
        k = kv[:, :HD]
        k = k * cosine + pltpu.roll(k, HD // 2, 1) * sine
        nkv[p, 0] = k.astype(bf16)
        nkv[p, 1] = kv[:, HD:].astype(bf16)

    owners = [owner_ref[c, n] for n in (n0, n1) for c in range(2)]

    def choose(d):
        block = 0
        for e in range(1, len(owners)):
            block = jnp.where(owners[e] == d, e, block)
        return block

    def push(k, _):
        d = lax.rem(g + k, groups)
        pbuf[d] = nkv[choose(d)]
        remote(pbuf.at[d], pushed_ref.at[g], ps_sem, pr_sem, (d, t)).start()
        return 0

    lax.fori_loop(1, groups, push, 0)
    pbuf[g] = nkv[choose(g)]
    keep = pltpu.make_async_copy(pbuf.at[g], pushed_ref.at[g], loc_sem.at[4 + chips])
    keep.start()

    arrived(3)
    attend(3, 0)
    attend(3, 1)

    def fresh_request(r, _):
        kn = jnp.concatenate([nkv[2 * r, 0], nkv[2 * r + 1, 0]], axis=0)
        vn = jnp.concatenate([nkv[2 * r, 1], nkv[2 * r + 1, 1]], axis=0)
        vn = jnp.concatenate([vn, jnp.ones_like(vn)], axis=1)
        causal = lax.broadcasted_iota(jnp.int32, (2 * BLK, 2 * BLK), 1) <= (
            lax.broadcasted_iota(jnp.int32, (2 * BLK, 2 * BLK), 0)
        )

        def step(s, _):
            scores = []
            for u in range(HEADS_PER_STEP):
                h = s * HEADS_PER_STEP + u
                q = qv[
                    pl.ds(pl.multiple_of(r * 2 * BLK, 2 * BLK), 2 * BLK),
                    pl.ds(pl.multiple_of(h * HD, HD), HD),
                ]
                sc = lax.dot_general(
                    q, kn, (((1,), (1,)), ((), ())), preferred_element_type=f32
                )
                scores.append(jnp.where(causal, sc, MASKED))
            for u in range(HEADS_PER_STEP):
                h = s * HEADS_PER_STEP + u
                i = r * heads + h
                old = m_ref[i]
                new = jnp.maximum(old, jnp.max(scores[u], axis=1, keepdims=True))
                alpha = jnp.exp2((old - new) * scale)
                w = jnp.exp2((scores[u] - new[:, :1]) * scale).astype(bf16)
                o = jnp.dot(w, vn, preferred_element_type=f32)
                total = acc_ref[i, :, HD:] * alpha + o[:, HD:]
                value = acc_ref[i, :, 0:HD] * alpha + o[:, :HD]
                att_ref[
                    pl.ds(pl.multiple_of(r * 2 * BLK, 2 * BLK), 2 * BLK),
                    pl.ds(pl.multiple_of(h * HD, HD), HD),
                ] = (value / total).astype(bf16)
            return 0

        lax.fori_loop(0, heads // HEADS_PER_STEP, step, 0)
        return 0

    lax.fori_loop(0, 2, fresh_request, 0)

    for p in range(pieces):
        own_right[p].wait_send()
        own_left[p].wait_send()
        exchange[p].wait_send()
    for f in forwards:
        f.wait_send()
    for rho in range(ROUNDS):
        drain(sbuf.at[rho, pl.ds(0, groups - 1)], as_sem.at[rho])
    keep.wait()
    drain(pbuf.at[pl.ds(0, groups - 1)], ps_sem)
    drain(pushed_ref.at[pl.ds(0, groups - 1)], pr_sem)


def per_device(
    hidden,
    queries,
    keyval_weight,
    keyval_pool,
    prefix_len,
    slot_request,
    hit_holder,
    hit_slot,
    new_owner,
    new_slot,
):
    groups = lax.axis_size("grp")
    rows, width = hidden.shape
    chips = lax.axis_size("tp") // 2
    pieces = rows // BLK
    heads = queries.shape[1] // HD
    pool_slots = keyval_pool.shape[0]
    pool = keyval_pool.reshape(pool_slots, 2, BLK, HD)
    weight = keyval_weight.reshape(-1, HD)

    frequency = ROPE_BASE ** (-(np.arange(HD // 2) * 2.0 / HD))
    frequency = jnp.asarray(np.concatenate([frequency, frequency])[None, :], f32)

    smem = pl.BlockSpec(memory_space=pltpu.SMEM)
    vmem = pl.BlockSpec(memory_space=pltpu.VMEM)
    anym = pl.BlockSpec(memory_space=pl.ANY)
    dma = pltpu.SemaphoreType.DMA
    V = pltpu.VMEM

    attention, pushed = pl.pallas_call(
        main_kernel,
        out_shape=(
            jax.ShapeDtypeStruct(queries.shape, bf16),
            jax.ShapeDtypeStruct((groups, 2, BLK, HD), bf16),
        ),
        in_specs=[smem, smem, smem, vmem, vmem, vmem, anym, anym, anym, anym],
        out_specs=(vmem, anym),
        scratch_shapes=[V((groups, 2, BLK, HD), bf16)] * ROUNDS
        + [
            V(pool.shape, bf16),
            V((ROUNDS, groups, 2, BLK, HD), bf16),
            V((4, groups, HD), jnp.int32),
            V((groups + MAXB, HD), jnp.int32),
            pltpu.SMEM((groups + MAXB, HD), jnp.int32),
            V(queries.shape, bf16),
            V((rows, width), bf16),
            V((pieces, BLK, width), bf16),
            V((pieces, BLK, width), bf16),
            V((pieces, BLK, width), bf16),
            V((chips, 2 * width, HD), bf16),
            V((chips, 2 * width, HD), bf16),
            V((WIDE + 8, HD), f32),
            V((chips, width, 2 * HD), bf16),
            V((chips, width, 2 * HD), bf16),
            V((rows, 2 * HD), f32),
            V((rows, 2 * HD), f32),
            V((rows, 2 * HD), f32),
            V((PER_ROUND * BLK, 2 * HD), bf16),
            V((PER_ROUND * BLK, 2 * HD), bf16),
            V((2 * heads, 2 * BLK, HD), f32),
            V((2 * heads, 2 * BLK, 2 * HD), f32),
            V((pieces, 2, BLK, HD), bf16),
            V((groups, 2, BLK, HD), bf16),
            dma((5 + chips,)),
            dma((chips,)),
            dma((chips,)),
            dma((pieces,)),
            dma((pieces,)),
            dma((pieces,)),
            dma((pieces,)),
            dma((2 * pieces,)),
            dma((pieces,)),
            dma((pieces,)),
            dma((ROUNDS,)),
            dma((ROUNDS,)),
            dma((pieces,)),
            dma((pieces,)),
            dma,
            dma,
        ],
        compiler_params=pltpu.CompilerParams(
            collective_id=0, has_side_effects=True, vmem_limit_bytes=62 * 2**20
        ),
    )(
        slot_request,
        prefix_len,
        new_owner.T,
        frequency,
        hit_holder,
        hit_slot,
        hidden,
        queries,
        weight,
        pool,
    )

    parts = 5
    new_pool = pl.pallas_call(
        store_kernel,
        out_shape=jax.ShapeDtypeStruct(pool.shape, bf16),
        in_specs=[smem, smem, smem, anym, anym],
        out_specs=anym,
        scratch_shapes=[
            V(pool.shape, bf16),
            V((groups, 2, BLK, HD), bf16),
            dma((parts,)),
            dma((parts,)),
            dma,
            dma((groups,)),
        ],
        compiler_params=pltpu.CompilerParams(vmem_limit_bytes=62 * 2**20),
    )(slot_request, new_owner.T, new_slot.T, pool, pushed)
    return attention, new_pool.reshape(keyval_pool.shape)


def solution(mesh):
    in_specs = (
        P("grp", "tp"),
        P("grp", "tp"),
        P(None, None, "tp"),
        P("grp", None, "tp", None, None),
        P(),
        P(),
        P(),
        P(),
        P(),
        P(),
    )
    out_specs = (P("grp", "tp"), P("grp", None, "tp", None, None))
    return jax.shard_map(
        per_device, mesh=mesh, in_specs=in_specs, out_specs=out_specs, check_vma=False
    )
```

time: 266 us -> 94.7 us (0.36)
  Pallas kernels: 236 us -> 92.7 us
  local copies, waits for them, and re-layouts: 21.2 us -> 1.15 us
  other arithmetic: 8.08 us -> 0 us
    pallas_call x2 -> x1, Pallas kernels: 141 us -> 6.19 us  [per_device(): pl.pallas_call(store_kernel, out_shape=jax.ShapeDtypeStruct(pool.shape, b...]
    unnamed x21 -> x3, local copies, waits for them, and re-layouts: 16.2 us -> 1.15 us
    pallas_call x1, Pallas kernels: 94.8 us -> 86.5 us  [per_device(): pl.pallas_call(main_kernel, out_shape=(jax.ShapeDtypeStruct(queries.shape...]
    gather x7 -> x0, local copies, waits for them, and re-layouts: 4.09 us -> none  [the longest x1 0.64 us: per_device(): lengths = prefix_len[my_requests]]
    reduce_sum x6 -> x0, other arithmetic: 3.68 us -> none  [the longest x1 1.95 us: tables(): jnp.sum(h0[:, None, None, :] <= holder[:, :, :, None], axis=-1, dtype=jnp...]
where the time goes in v2:
time: 94.7 us; the launch traced here: 94.5 us
  Pallas kernels  92.7 us (98%)
  local copies, waits for them, and re-layouts  1.15 us (1%)
    pallas_call x1, Pallas kernels, per_device(): pl.pallas_call(main_kernel, out_shape=(jax.ShapeDtypeStruct(queries.shape...  86.5 us
    pallas_call x1, Pallas kernels, per_device(): pl.pallas_call(store_kernel, out_shape=jax.ShapeDtypeStruct(pool.shape, b...  6.19 us

profile of v2, /device:TPU:1, one launch (start us, length us, event | category | flops | bytes accessed | tf_op | source)
XLA Modules:
  0.0 94.5 jit_solution(7390232868578492800)
XLA Ops:
  0.6 86.5 %shard_map.122 = (bf16[512,1536]{1,0:T(8,128)(2,1)}, bf16[16,2,128,128]{3,2,1,0:T(8,128)(2,1)}) custom-call(s32[32]{0:T(128)} %request_ref.3, s32[32]{0:T(128)} %length_ref.1, s32[2,32]{1,0:T(2,128)} %bitcast.11, f32[1,128]{1,0:T(1,128)} %constant.2.clone.freq_ref, s32[32,32]{1,0:T(8,128)} %holder_ref.1, s32[32,32]{1,0:T(8,128)} %slot_ref.1, ...), custom_call_target="tpu_custom_call" | custom-call | tf_op jit(solution)/shard_map/pallas_call | solution.py:597
  87.1 0.0 copy-start
  87.2 6.2 %shard_map.123 = bf16[80,2,128,128]{3,2,1,0:T(8,128)(2,1)} custom-call(s32[32]{0:T(128)} %request_ref.3, s32[2,32]{1,0:T(2,128)} %bitcast.12, s32[2,32]{1,0:T(2,128)} %bitcast.13, bf16[80,2,128,128]{3,2,1,0:T(8,128)(2,1)} %bitcast.8, bf16[16,2,128,128]{3,2,1,0:T(8,128)(2,1)} %get-tuple-element.5.pushed_ref), custom_call_target="tpu_custom_call" | custom-call | tf_op jit(solution)/shard_map/pallas_call | solution.py:665
  93.4 0.0 copy-done
  93.4 1.1 %copy.15 = bf16[512,1536]{1,0:T(8,128)(2,1)} copy(bf16[512,1536]{1,0:T(8,128)(2,1)S(1)} %copy-done) | data formatting | bytes 3145728
Async XLA Ops:
  87.1 6.2 %copy-start = (bf16[512,1536]{1,0:T(8,128)(2,1)S(1)}, bf16[512,1536]{1,0:T(8,128)(2,1)}, u32[]{:S(2)}) copy-start(bf16[512,1536]{1,0:T(8,128)(2,1)} %get-tuple-element.10) | copy-start | bytes 4718596
